TPU v7x, 32 devices: a whole 2x2x4 slice. The times are simulated.
32 devices in a mesh: dp: 4 (over z), expert: 2 (over x), head: 4 (over y, core).
Axes of the slice: x: 2, y: 2, z: 4, core: 2. Of those that a mesh axis runs over, the one named last changes fastest.
Arguments:
- hidden_in: bfloat16 [1024, 7168], P(('dp', 'expert'), 'head'), may hold values from -6 to 6
- grad_out: bfloat16 [1024, 7168], P(('dp', 'expert'), 'head'), may hold values from -6 to 6
- expert_ids: int32 [1024, 8], P(('dp', 'expert')), may hold values from 0 to 255, all different within a row; in each aligned block of 128 rows (0 to 127, 128 to 255, ...) at most 8 rows name the same one
- gate_weights: float32 [1024, 8], P(('dp', 'expert')), may hold values from 0.1 to 1
- w_gate: bfloat16 [8, 7168, 2048], P(('dp', 'expert'), None, 'head'), may hold values from -0.0625 to 0.0625
- w_up: bfloat16 [8, 7168, 2048], P(('dp', 'expert'), None, 'head'), may hold values from -0.0625 to 0.0625
- w_down: bfloat16 [8, 2048, 7168], P(('dp', 'expert'), 'head'), may hold values from -0.125 to 0.125
- latent_kv: bfloat16 [1024, 576], P(('dp', 'expert')), may hold values from -16 to 16
- query: bfloat16 [1024, 12288], P('dp', ('expert', 'head')), may hold values from -240 to 240
- d_attn: bfloat16 [1024, 8192], P('dp', ('expert', 'head')), may hold values from -6 to 6
- w_uk: bfloat16 [512, 8192], P(None, ('expert', 'head')), may hold values from -0.25 to 0.25
- w_uv: bfloat16 [512, 8192], P(None, ('expert', 'head')), may hold values from -0.25 to 0.25
- doc_ids: int32 [1024], P('dp'), may hold values from 0 to 15, never falling along the last dimension, each value on 1 to 256 neighbouring positions
Outputs:
- d_hidden: bfloat16 [1024, 7168], P(('dp', 'expert'), 'head')
- d_gates: bfloat16 [1024, 8], P(('dp', 'expert'))
- d_query: bfloat16 [1024, 12288], P('dp', ('expert', 'head'))
- d_latent_kv: bfloat16 [1024, 576], P(('dp', 'expert'), 'head')
Inputs may be any that keep to these rules, and one draw needn't show every extreme that they name: `expert_ids`: each row names 8 different experts; in each aligned block of 128 rows (the rows of one device) no expert is named by more than 8 rows, a bound that some block reaches. `doc_ids`: document numbers never fall; each document has 1 to 256 tokens.
All inputs are finite; a program needn't handle non-finite values.
Results may differ from a plain program's by a relative error of at most 0.0089.
Values may be sent and summed in bfloat16 or wider, within the bound.
A program may use at most 128 MiB of HBM per device.

v0:
```python
import math
import jax
import jax.numpy as jnp
from jax import lax
from jax.sharding import PartitionSpec as P

TOP = 8
LAT = 512
NOPE = 128
ROPE = 64
VD = 128
CAP = 8
CONTRACT_LAST = (((1,), (1,)), ((), ()))


def expert_backward(rows_x, rows_dy, gate_mat, up_mat, down_mat):
    gate_pre = jnp.dot(rows_x, gate_mat, preferred_element_type=jnp.float32)
    up_pre = jnp.dot(rows_x, up_mat, preferred_element_type=jnp.float32)
    back_hidden = lax.dot_general(
        rows_dy, down_mat, CONTRACT_LAST, preferred_element_type=jnp.float32
    )
    sig_val = jax.nn.sigmoid(gate_pre)
    act_val = gate_pre * sig_val
    gate_part = jnp.sum(act_val * up_pre * back_hidden, axis=1)
    d_up = (back_hidden * act_val).astype(jnp.bfloat16)
    d_pre = (back_hidden * up_pre * sig_val * (1.0 + gate_pre * (1.0 - sig_val))).astype(
        jnp.bfloat16
    )
    row_part = lax.dot_general(
        d_pre, gate_mat, CONTRACT_LAST, preferred_element_type=jnp.float32
    ) + lax.dot_general(d_up, up_mat, CONTRACT_LAST, preferred_element_type=jnp.float32)
    return (row_part, gate_part)


def expert_half(hidden_in, grad_out, expert_ids, gate_weights, w_gate, w_up, w_down):
    window_size = lax.axis_size("dp") * lax.axis_size("expert")
    head_count = lax.axis_size("head")
    tok_local = expert_ids.shape[0]
    route_count = tok_local * TOP
    flat_ids = expert_ids.reshape(route_count)
    inside = flat_ids < window_size
    one_hot = (flat_ids[:, None] == jnp.arange(window_size, dtype=jnp.int32)[None, :]).astype(
        jnp.int32
    )
    earlier = jnp.cumsum(one_hot, axis=0) - one_hot
    slot_num = jnp.sum(earlier * one_hot, axis=1)
    target = jnp.where(inside, flat_ids * CAP + slot_num, window_size * CAP)
    slot_hits = target[None, :] == jnp.arange(window_size * CAP, dtype=jnp.int32)[:, None]
    filled = jnp.any(slot_hits, axis=1)
    route_of_slot = jnp.sum(
        jnp.where(slot_hits, jnp.arange(route_count, dtype=jnp.int32)[None, :], 0), axis=1
    )
    token_of_slot = route_of_slot // TOP
    rows_x, rows_dy = (hidden_in, grad_out)
    send_x = jnp.where(filled[:, None], jnp.take(rows_x, token_of_slot, axis=0), 0)
    send_dy = jnp.where(filled[:, None], jnp.take(rows_dy, token_of_slot, axis=0), 0)
    send_x = send_x.reshape(window_size, CAP, send_x.shape[1])
    send_dy = send_dy.reshape(window_size, CAP, send_dy.shape[1])
    got_x = lax.all_to_all(send_x, ("dp", "expert"), split_axis=0, concat_axis=0, tiled=True)
    got_dy = lax.all_to_all(send_dy, ("dp", "expert"), split_axis=0, concat_axis=0, tiled=True)
    got_x, got_dy = (
        lax.all_gather(got_x, "head", axis=2, tiled=True),
        lax.all_gather(got_dy, "head", axis=2, tiled=True),
    )
    sources = got_x.shape[0]
    items = got_x.shape[1]
    flat_x = got_x.reshape(sources * items, got_x.shape[2])
    flat_dy = got_dy.reshape(sources * items, got_dy.shape[2])
    row_part, gate_part = expert_backward(flat_x, flat_dy, w_gate[0], w_up[0], w_down[0])
    gate_spread = jnp.broadcast_to(gate_part[:, None], (sources * items, head_count))
    summed = lax.psum_scatter(row_part, "head", scatter_dimension=1, tiled=True)
    gate_sum = lax.psum_scatter(gate_spread, "head", scatter_dimension=1, tiled=True)
    back_rows = summed.astype(jnp.bfloat16).reshape(sources, items, summed.shape[1])
    back_gate = gate_sum[:, 0].astype(jnp.bfloat16).reshape(sources, items)
    back_rows, back_gate = (
        lax.all_to_all(back_rows, ("dp", "expert"), split_axis=0, concat_axis=0, tiled=True),
        lax.all_to_all(back_gate, ("dp", "expert"), split_axis=0, concat_axis=0, tiled=True),
    )
    flat_back = back_rows.reshape(window_size * CAP, back_rows.shape[2])
    flat_gate = back_gate.reshape(window_size * CAP)
    safe_target = jnp.where(inside, target, 0)
    route_weight = jnp.where(inside, gate_weights.reshape(route_count), 0.0)
    picked = jnp.take(flat_back, safe_target, axis=0).astype(jnp.float32) * route_weight[:, None]
    d_hidden = jnp.sum(picked.reshape(tok_local, TOP, picked.shape[1]), axis=1).astype(jnp.bfloat16)
    d_gates = jnp.where(inside, jnp.take(flat_gate, safe_target), jnp.zeros((), jnp.bfloat16))
    return (d_hidden, d_gates.reshape(tok_local, TOP))


def attention_half(latent_kv, query, d_attn, w_uk, w_uv, doc_ids):
    seq_len = query.shape[0]
    heads_here = w_uk.shape[1] // NOPE
    score_scale = 1.0 / math.sqrt(NOPE + ROPE)
    w_both = jnp.concatenate([w_uk, w_uv], axis=1)
    piece = lax.all_gather(latent_kv, "expert", axis=0, tiled=True)
    lifted = jnp.dot(piece[:, :LAT], w_both, preferred_element_type=jnp.float32).astype(
        jnp.bfloat16
    )
    keyvals = jnp.concatenate([lifted, piece[:, LAT:]], axis=1)
    key_nope = keyvals[:, : heads_here * NOPE].reshape(seq_len, heads_here, NOPE)
    all_values = keyvals[:, heads_here * NOPE : heads_here * (NOPE + VD)].reshape(
        seq_len, heads_here, VD
    )
    rope_key = keyvals[:, heads_here * (NOPE + VD) :]
    all_keys = jnp.concatenate(
        [key_nope, jnp.broadcast_to(rope_key[:, None, :], (seq_len, heads_here, ROPE))], axis=2
    )
    queries = query.reshape(seq_len, heads_here, NOPE + ROPE)
    douts = d_attn.reshape(seq_len, heads_here, VD)
    positions = jnp.arange(seq_len, dtype=jnp.int32)
    block_rows = min(512, seq_len)
    dkey_sum = jnp.zeros((seq_len, heads_here, NOPE + ROPE), jnp.float32)
    dval_sum = jnp.zeros((seq_len, heads_here, VD), jnp.float32)
    dq_blocks = []
    for block_num in range(seq_len // block_rows):
        first_row = block_num * block_rows
        query_blk = queries[first_row : first_row + block_rows]
        dout_blk = douts[first_row : first_row + block_rows]
        scores = (
            jnp.einsum("qhd,khd->hqk", query_blk, all_keys, preferred_element_type=jnp.float32)
            * score_scale
        )
        allowed = (positions[None, :] <= positions[first_row : first_row + block_rows, None]) & (
            doc_ids[None, :] == doc_ids[first_row : first_row + block_rows, None]
        )
        scores = jnp.where(allowed[None], scores, -1e30)
        top_score = jnp.max(scores, axis=2, keepdims=True)
        expd = jnp.exp(scores - top_score)
        probs = expd / jnp.sum(expd, axis=2, keepdims=True)
        dprobs = jnp.einsum(
            "qhd,khd->hqk", dout_blk, all_values, preferred_element_type=jnp.float32
        )
        inner = jnp.sum(probs * dprobs, axis=2, keepdims=True)
        dscore = (probs * (dprobs - inner) * score_scale).astype(jnp.bfloat16)
        prob_low = probs.astype(jnp.bfloat16)
        dq_blocks.append(
            jnp.einsum("hqk,khd->qhd", dscore, all_keys, preferred_element_type=jnp.float32).astype(
                jnp.bfloat16
            )
        )
        dkey_sum = dkey_sum + jnp.einsum(
            "hqk,qhd->khd", dscore, query_blk, preferred_element_type=jnp.float32
        )
        dval_sum = dval_sum + jnp.einsum(
            "hqk,qhd->khd", prob_low, dout_blk, preferred_element_type=jnp.float32
        )
    d_query = jnp.concatenate(dq_blocks, axis=0).reshape(seq_len, heads_here * (NOPE + ROPE))
    dkey_low = dkey_sum.astype(jnp.bfloat16)
    dval_low = dval_sum.astype(jnp.bfloat16)
    row_count = lax.axis_size("expert") * latent_kv.shape[0]
    nope_flat = dkey_low[:, :, :NOPE].reshape(row_count, heads_here * NOPE)
    lat_term = lax.dot_general(
        nope_flat, w_uk, CONTRACT_LAST, preferred_element_type=jnp.float32
    ) + lax.dot_general(
        dval_low.reshape(row_count, heads_here * VD),
        w_uv,
        CONTRACT_LAST,
        preferred_element_type=jnp.float32,
    )
    rope_term = jnp.sum(dkey_low[:, :, NOPE:].astype(jnp.float32), axis=1)
    own_rows = lax.psum_scatter(
        jnp.concatenate([lat_term, rope_term], axis=1), "expert", scatter_dimension=0, tiled=True
    )
    d_latent = lax.psum_scatter(own_rows, "head", scatter_dimension=1, tiled=True)
    return (d_query, d_latent.astype(jnp.bfloat16))


def body(
    hidden_in,
    grad_out,
    expert_ids,
    gate_weights,
    w_gate,
    w_up,
    w_down,
    latent_kv,
    query,
    d_attn,
    w_uk,
    w_uv,
    doc_ids,
):
    d_query, d_latent_kv = attention_half(latent_kv, query, d_attn, w_uk, w_uv, doc_ids)
    d_hidden, d_gates = expert_half(
        hidden_in, grad_out, expert_ids, gate_weights, w_gate, w_up, w_down
    )
    return (d_hidden, d_gates, d_query, d_latent_kv)


def solution(mesh):
    placed = (
        P(("dp", "expert"), "head"),
        P(("dp", "expert"), "head"),
        P(("dp", "expert"), None),
        P(("dp", "expert"), None),
        P(("dp", "expert"), None, "head"),
        P(("dp", "expert"), None, "head"),
        P(("dp", "expert"), "head", None),
        P(("dp", "expert"), None),
        P("dp", ("expert", "head")),
        P("dp", ("expert", "head")),
        P(None, ("expert", "head")),
        P(None, ("expert", "head")),
        P("dp"),
    )
    return jax.shard_map(
        body,
        mesh=mesh,
        in_specs=placed,
        out_specs=(
            P(("dp", "expert"), "head"),
            P(("dp", "expert"), None),
            P("dp", ("expert", "head")),
            P(("dp", "expert"), "head"),
        ),
        check_vma=False,
    )
```

profile of v0, /device:TPU:0, one launch (start us, length us, event | category | flops | bytes accessed | tf_op | source)
XLA Modules:
  0.0 199.1 jit_solution(16776576463837883362)
XLA Ops:
  8.3 2.3 %reduce-window.6 = s32[8,8,128]{2,1,0:T(8,128)S(1)} reduce-window(s32[8,8,128]{2,1,0:T(8,128)S(1)} %fusion.39, s32[]{:T(128)} %constant.44.clone.1), window={size=1x1x128 pad=0_0x0_0x127_0}, to_apply=%region_0.1 | reduce-window | flops 1040384 | bytes 65540 | tf_op jit(solution)/shard_map/reduce-window
  13.8 7.3 %all-to-all-start.1 = ((bf16[8,8,1792]{2,1,0:T(8,128)(2,1)}), bf16[8,8,1792]{2,1,0:T(8,128)(2,1)S(1)}, u32[]{:S(2)}, u32[]{:S(2)}) async-start(bf16[8,8,1792]{2,1,0:T(8,128)(2,1)} %get-tuple-element.34), calls=%async_computation.1 | async-start | bytes 458752 | tf_op jit(solution)/shard_map/all_to_all | solution.py:59
  21.3 7.8 %all_gather.11 = bf16[256,576]{0,1:T(8,128)(2,1)S(1)} all-gather(bf16[128,576]{0,1:T(8,128)(2,1)S(1)} %copy-done.5), channel_id=1, replica_groups=mesh['dp'=4,'expert'=2,'head'=4] {'expert'}, dimensions={0}, use_global_device_ids=true | all-gather | bytes 442368 | tf_op jit(solution)/shard_map/all_gather | solution.py:94
  30.5 2.0 fusion.11
  37.4 3.6 %fusion.60 = (f32[8,256]{1,0:T(8,128)S(1)}, f32[8,256,256]{1,2,0:T(8,128)}) fusion(pred[256,256]{0,1:T(8,128)(4,1)S(1)} %fusion.31, bf16[256,8,192]{0,2,1:T(8,128)(2,1)} %bitcast.185, bf16[256,8,64]{0,2,1:T(8,128)(2,1)} %broadcast_in_dim.128, bf16[256,8,128]{0,2,1:T(8,128)(2,1)} %bitcast.188), kind=kOutput, calls=%fused_computation.174 | convolution fusion | flops 204996864 | bytes 3743744 | tf_op jit(solution)/shard_map/sub | solution.py:127
  41.0 2.9 %convolution_convert_fusion.3 = bf16[8,256,128]{1,2,0:T(8,128)(2,1)} fusion(bf16[256,8,128]{0,2,1:T(8,128)(2,1)S(1)} %bitcast.180, f32[8,256,256]{1,2,0:T(8,128)} %get-tuple-element.102, f32[8,256]{1,0:T(8,128)S(1)} %get-tuple-element.101), kind=kOutput, calls=%fused_computation.32 | convolution fusion | flops 135528448 | bytes 3153920 | tf_op jit(solution)/shard_map/hqk,qhd->khd/dot_general | solution.py:143
  43.9 4.2 %fusion.19 = bf16[256,8,192]{0,2,1:T(8,128)(2,1)} fusion(bf16[256,8,192]{0,2,1:T(8,128)(2,1)} %bitcast.186, f32[8,256,256]{2,1,0:T(8,128)S(1)} %fusion.61, f32[8,256,256]{1,2,0:T(8,128)} %get-tuple-element.102, f32[8,256]{1,0:T(8,128)S(1)} %get-tuple-element.101), kind=kOutput, calls=%fused_computation.33 | convolution fusion | flops 205392128 | bytes 5775360 | tf_op jit(solution)/shard_map/hqk,qhd->khd/dot_general | solution.py:140
  53.4 1.9 convolution_add_fusion.1
  56.2 4.8 %all-to-all-start = ((bf16[8,8,1792]{2,1,0:T(8,128)(2,1)}), bf16[8,8,1792]{2,1,0:T(8,128)(2,1)S(1)}, u32[]{:S(2)}, u32[]{:S(2)}) async-start(bf16[8,8,1792]{2,1,0:T(8,128)(2,1)} %get-tuple-element.33), calls=%async_computation | async-start | bytes 458752 | tf_op jit(solution)/shard_map/all_to_all | solution.py:60
  61.1 9.5 %all_gather.10 = bf16[8,8,7168]{2,1,0:T(8,128)(2,1)S(1)} all-gather(bf16[8,8,1792]{2,1,0:T(8,128)(2,1)S(1)} %all-to-all-done.1), channel_id=1, replica_groups=mesh['dp'=4,'expert'=2,'head'=4] {'head'}, dimensions={2}, use_global_device_ids=true | all-gather | bytes 1146880 | tf_op jit(solution)/shard_map/all_gather | solution.py:62
  70.5 4.6 %fusion.4 = f32[64,512]{1,0:T(8,128)S(1)} fusion(bf16[1,7168,512]{2,1,0:T(8,128)(2,1)} %param.19, bf16[8,8,7168]{2,1,0:T(8,128)(2,1)S(1)} %all_gather.10), kind=kOutput, calls=%fused_computation.8 | convolution fusion | flops 469762048 | bytes 8388608 | tf_op jit(solution)/shard_map/dot_general | solution.py:17
  76.6 9.6 %all_gather.9 = bf16[8,8,7168]{2,1,0:T(8,128)(2,1)S(1)} all-gather(bf16[8,8,1792]{2,1,0:T(8,128)(2,1)S(1)} %all-to-all-done), channel_id=1, replica_groups=mesh['dp'=4,'expert'=2,'head'=4] {'head'}, dimensions={2}, use_global_device_ids=true | all-gather | bytes 1146880 | tf_op jit(solution)/shard_map/all_gather | solution.py:63
  86.2 5.7 %multiply_reduce_fusion.1 = (f32[64]{0:T(128)S(1)}, f32[64,512]{1,0:T(8,128)S(1)}) fusion(f32[64,512]{1,0:T(8,128)S(1)} %fusion.7, f32[64,512]{1,0:T(8,128)S(1)} %fusion.4, bf16[1,512,7168]{2,1,0:T(8,128)(2,1)} %param.21, bf16[8,8,7168]{2,1,0:T(8,128)(2,1)S(1)} %all_gather.9), kind=kOutput, calls=%fused_computation.60 | convolution fusion | flops 469991360 | bytes 8651008 | tf_op jit(solution)/shard_map/dot_general | solution.py:19
  91.9 5.5 %fusion.2 = f32[64,7168]{1,0:T(8,128)S(1)} fusion(bf16[1,7168,512]{2,1,0:T(8,128)(2,1)} %param.19, f32[64,512]{1,0:T(8,128)S(1)} %fusion.4, f32[64,512]{1,0:T(8,128)S(1)} %get-tuple-element.100, f32[64,512]{1,0:T(8,128)S(1)} %fusion.7), kind=kOutput, calls=%fused_computation.6 | convolution fusion | flops 470089728 | bytes 9568256 | tf_op jit(solution)/shard_map/dot_general | solution.py:29
  97.5 3.6 %convolution_add_fusion = f32[64,7168]{1,0:T(8,128)} fusion(f32[64,7168]{1,0:T(8,128)S(1)} %fusion.2, bf16[1,7168,512]{2,1,0:T(8,128)(2,1)S(1)} %bitcast.178, f32[64,512]{1,0:T(8,128)S(1)} %get-tuple-element.100, f32[64,512]{1,0:T(8,128)S(1)} %fusion.4), kind=kOutput, calls=%fused_computation.5 | convolution fusion | flops 470417408 | bytes 11272192 | tf_op jit(solution)/shard_map/dot_general | solution.py:31
  102.3 3.3 %convolution_convert_fusion.2 = bf16[8,192,256]{2,1,0:T(8,128)(2,1)S(1)} fusion(f32[8,256,256]{2,1,0:T(8,128)S(1)} %fusion.61, bf16[256,8,64]{0,2,1:T(8,128)(2,1)} %broadcast_in_dim.128, bf16[256,8,128]{0,2,1:T(8,128)(2,1)} %bitcast.189, f32[8,256,256]{1,2,0:T(8,128)} %get-tuple-element.102, f32[8,256]{1,0:T(8,128)S(1)} %get-tuple-element.101), kind=kOutput, calls=%fused_computation.31 | convolution fusion | flops 206964992 | bytes 5775360 | tf_op jit(solution)/shard_map/hqk,khd->qhd/dot_general | solution.py:136
  105.7 6.4 %all-reduce = bf16[64,4]{0,1:T(4,128)(2,1)S(1)} all-reduce(f32[64,4]{0,1:T(4,128)S(1)} %broadcast_in_dim.125), channel_id=3, replica_groups=mesh['dp'=4,'expert'=2,'head'=4] {'head'}, use_global_device_ids=true, to_apply=%region_8.10.clone | all-reduce | flops 256 | bytes 1536
  113.5 5.7 %all-to-all-start.3 = ((bf16[8,1,8]{2,1,0:T(2,128)(2,1)}), bf16[8,1,8]{2,1,0:T(2,128)(2,1)S(1)}, u32[]{:S(2)}, u32[]{:S(2)}) async-start(bf16[8,1,8]{2,1,0:T(2,128)(2,1)} %convert_element_type.97), calls=%async_computation.4 | async-start | bytes 8192 | tf_op jit(solution)/shard_map/all_to_all | solution.py:77
  120.4 5.1 %all-to-all-done.3 = bf16[8,1,8]{2,1,0:T(2,128)(2,1)S(1)} async-done(((bf16[8,1,8]{2,1,0:T(2,128)(2,1)}), bf16[8,1,8]{2,1,0:T(2,128)(2,1)S(1)}, u32[]{:S(2)}, u32[]{:S(2)}) %all-to-all-start.3) | async-done | bytes 160 | tf_op jit(solution)/shard_map/all_to_all | solution.py:77
  128.5 1.8 copy.104
  133.3 5.5 %all-to-all-start.2 = ((bf16[8,8,1792]{2,1,0:T(8,128)(2,1)}), bf16[8,8,1792]{2,1,0:T(8,128)(2,1)S(1)}, u32[]{:S(2)}, u32[]{:S(2)}) async-start(bf16[8,8,1792]{2,1,0:T(8,128)(2,1)} %convert_bitcast_fusion), calls=%async_computation.3 | async-start | bytes 458752 | tf_op jit(solution)/shard_map/all_to_all | solution.py:76
  138.8 39.9 %compare_select_fusion.2 = bf16[1024]{0:T(1024)(128)(2,1)S(1)} fusion(s32[1024]{0:T(1024)S(1)} %bitcast.193, bf16[]{:T(256)} %bitcast.13, bf16[]{:T(256)} %bitcast.14, bf16[]{:T(256)} %bitcast.15, bf16[]{:T(256)} %bitcast.16, bf16[]{:T(256)} %bitcast.17, bf16[]{:T(256)} %bitcast.18, bf16[]{:T(256)} %bitcast.19, bf16[]{:T(256)} %bitcast.20, bf16[]{:T(256)} %bitcast.21, ...), kind=kLoop, calls=%fused_computation.85 | loop fusion | flops 129024 | bytes 6272 | tf_op jit(solution)/shard_map/jit(_take)/gather | solution.py:85
  181.2 5.8 %gather_fusion = bf16[1024,1792]{1,0:T(8,128)(2,1)} fusion(bf16[64,1792]{1,0:T(8,128)(2,1)S(1)} %bitcast.174, s32[1024]{0:T(1024)S(1)} %broadcast_clamp_fusion), kind=kCustom, calls=%fused_computation.2 | custom fusion | bytes 7344128 | tf_op jit(solution)/shard_map/jit(_take)/gather | solution.py:83
  187.0 5.6 %multiply_reduce_fusion = bf16[128,1792]{1,0:T(8,128)(2,1)} fusion(bf16[1024,1792]{1,0:T(8,128)(2,1)} %gather_fusion, f32[128,8]{1,0:T(8,128)S(1)} %get-tuple-element.27, pred[128,8]{1,0:T(8,128)(4,1)S(1)} %get-tuple-element.26), kind=kLoop, calls=%fused_computation.15 | loop fusion | flops 7110656 | bytes 4133888 | tf_op jit(solution)/shard_map/reduce_sum | solution.py:84
  (95 shorter events, 30.6 us)
Async XLA Ops:
  7.2 4.2 %copy-start = (bf16[128,1792]{1,0:T(8,128)(2,1)S(1)}, bf16[128,1792]{1,0:T(8,128)(2,1)}, u32[]{:S(2)}) copy-start(bf16[128,1792]{1,0:T(8,128)(2,1)} %param.15) | copy-start | bytes 1376260
  7.2 5.0 %copy-start.1 = (bf16[128,1792]{1,0:T(8,128)(2,1)S(1)}, bf16[128,1792]{1,0:T(8,128)(2,1)}, u32[]{:S(2)}) copy-start(bf16[128,1792]{1,0:T(8,128)(2,1)} %param.16) | copy-start | bytes 1376260
  12.2 9.0 %copy-start.7 = (s32[256]{0:T(256)S(1)}, s32[256]{0:T(256)}, u32[]{:S(2)}) copy-start(s32[256]{0:T(256)} %param.27) | copy-start | bytes 3076
  12.2 9.1 %copy-start.5 = (bf16[128,576]{0,1:T(8,128)(2,1)S(1)}, bf16[128,576]{0,1:T(8,128)(2,1)}, u32[]{:S(2)}) copy-start(bf16[128,576]{0,1:T(8,128)(2,1)} %param.22) | copy-start | bytes 442372
  12.2 18.3 %copy-start.2 = (bf16[512,1024]{1,0:T(8,128)(2,1)S(1)}, bf16[512,1024]{1,0:T(8,128)(2,1)}, u32[]{:S(2)}) copy-start(bf16[512,1024]{1,0:T(8,128)(2,1)} %param.25) | copy-start | bytes 3145732
  13.8 42.4 %all-to-all-start.1 = ((bf16[8,8,1792]{2,1,0:T(8,128)(2,1)}), bf16[8,8,1792]{2,1,0:T(8,128)(2,1)S(1)}, u32[]{:S(2)}, u32[]{:S(2)}) async-start(bf16[8,8,1792]{2,1,0:T(8,128)(2,1)} %get-tuple-element.34), calls=%async_computation.1 | async-start | bytes 458752 | tf_op jit(solution)/shard_map/all_to_all | solution.py:59
  21.1 107.4 %reduce-scatter.8.cloned.1.call-start = ((), (), s32[]{:S(2)}) async-start(), calls=%async_computation.8 | async-start | bytes 983040 | tf_op jit(solution)/shard_map/reduce_scatter | solution.py:160
  29.1 1.4 copy-start.4
  32.5 1.5 copy-start.3
  34.0 2.7 %slice-start.4 = ((bf16[256,576]{0,1:T(8,128)(2,1)}), bf16[256,64]{0,1:T(8,128)(2,1)S(1)}, s32[]{:S(2)}) async-start(bf16[256,576]{0,1:T(8,128)(2,1)} %copy-done.4), calls=%async_computation.14 | async-start | bytes 65536 | tf_op jit(solution)/shard_map/slice | solution.py:98
  56.2 20.4 %all-to-all-start = ((bf16[8,8,1792]{2,1,0:T(8,128)(2,1)}), bf16[8,8,1792]{2,1,0:T(8,128)(2,1)S(1)}, u32[]{:S(2)}, u32[]{:S(2)}) async-start(bf16[8,8,1792]{2,1,0:T(8,128)(2,1)} %get-tuple-element.33), calls=%async_computation | async-start | bytes 458752 | tf_op jit(solution)/shard_map/all_to_all | solution.py:60
  61.0 70.5 %reduce-scatter.6.cloned.1.call-start = ((), (), s32[]{:S(2)}) async-start(), calls=%async_computation.7 | async-start | bytes 2293760 | tf_op jit(solution)/shard_map/reduce_scatter | solution.py:71
  61.1 14.1 %slice-start = ((s8[7340032]{0:T(1024)(128)(4,1)}), s8[4194304]{0:T(1024)(128)(4,1)S(1)}, s32[]{:S(2)}) async-start(s8[7340032]{0:T(1024)(128)(4,1)} %bitcast.175), calls=%async_computation.10 | async-start | bytes 8388608
  70.5 4.7 %slice-start.1 = ((s8[7340032]{0:T(1024)(128)(4,1)}), s8[3145728]{0:T(1024)(128)(4,1)S(1)}, s32[]{:S(2)}) async-start(s8[7340032]{0:T(1024)(128)(4,1)} %bitcast.175), calls=%async_computation.11 | async-start | bytes 6291456
  86.2 11.3 %slice-start.2 = ((s8[7340032]{0:T(1024)(128)(4,1)}), s8[4194304]{0:T(1024)(128)(4,1)S(1)}, s32[]{:S(2)}) async-start(s8[7340032]{0:T(1024)(128)(4,1)} %bitcast.177), calls=%async_computation.12 | async-start | bytes 8388608
  91.9 5.6 %slice-start.3 = ((s8[7340032]{0:T(1024)(128)(4,1)}), s8[3145728]{0:T(1024)(128)(4,1)S(1)}, s32[]{:S(2)}) async-start(s8[7340032]{0:T(1024)(128)(4,1)} %bitcast.177), calls=%async_computation.13 | async-start | bytes 6291456
  97.5 3.7 %copy-start.6 = (f32[128,8]{0,1:T(8,128)S(1)}, f32[128,8]{0,1:T(8,128)}, u32[]{:S(2)}) copy-start(f32[128,8]{0,1:T(8,128)} %param.18) | copy-start | bytes 12292
  101.1 0.7 copy-start.8
  113.5 12.1 %all-to-all-start.3 = ((bf16[8,1,8]{2,1,0:T(2,128)(2,1)}), bf16[8,1,8]{2,1,0:T(2,128)(2,1)S(1)}, u32[]{:S(2)}, u32[]{:S(2)}) async-start(bf16[8,1,8]{2,1,0:T(2,128)(2,1)} %convert_element_type.97), calls=%async_computation.4 | async-start | bytes 8192 | tf_op jit(solution)/shard_map/all_to_all | solution.py:77
  119.1 60.3 %reduce-scatter.10.cloned.1.call-start = ((), (), s32[]{:S(2)}) async-start(), calls=%async_computation.9 | async-start | bytes 368640
  133.3 47.9 %all-to-all-start.2 = ((bf16[8,8,1792]{2,1,0:T(8,128)(2,1)}), bf16[8,8,1792]{2,1,0:T(8,128)(2,1)S(1)}, u32[]{:S(2)}, u32[]{:S(2)}) async-start(bf16[8,8,1792]{2,1,0:T(8,128)(2,1)} %convert_bitcast_fusion), calls=%async_computation.3 | async-start | bytes 458752 | tf_op jit(solution)/shard_map/all_to_all | solution.py:76
Sparse Core Ops, SparseCore 0:
  56.3 18.3 reduce-scatter.7
  101.2 30.2 reduce-scatter.5
  134.6 20.2 reduce-scatter.9
where the time goes:
time: 201 us; the launch traced here: 199 us
  other arithmetic  53.6 us (27%)
  matrix products  41.9 us (21%)
  blocking collectives  33.3 us (17%)
  local copies, waits for them, and re-layouts  26.4 us (13%)
  starting transfers between devices  23.3 us (12%)
  between operations  14.2 us (7%)
  waiting for transfers between devices  6.3 us (3%)
    gather x1, other arithmetic, expert_half(): jnp.take(flat_gate, safe_target)  39.9 us
    all_gather x1, blocking collectives, expert_half(): lax.all_gather(got_dy, 'head', axis=2, tiled=True)  9.6 us
    all_gather x1, blocking collectives, expert_half(): lax.all_gather(got_x, 'head', axis=2, tiled=True)  9.47 us
    unnamed x35, local copies, waits for them, and re-layouts  8.81 us
    all_gather x1, blocking collectives, attention_half(): piece = lax.all_gather(latent_kv, 'expert', axis=0, tiled=True)  7.85 us
    all_to_all x1, starting transfers between devices, expert_half(): lax.all_to_all(send_x, ('dp', 'expert'), split_axis=0, concat_axis=0, til...  7.25 us
    unnamed x1, blocking collectives  6.42 us
    gather x1, local copies, waits for them, and re-layouts, expert_half(): jnp.take(flat_back, safe_target, axis=0).astype(jnp.float32)  5.82 us
  transfers between devices with their start and end apart: 7, of which 2 were waited for; matrix products, arithmetic and copies ran while one was open for 52% of the time, Pallas kernels for 0%

commit v1 on v0

--- a/solution.py
+++ b/solution.py
@@ -11,6 +11,19 @@
 VD = 128
 CAP = 8
 CONTRACT_LAST = (((1,), (1,)), ((), ()))
+
+
+def ring_gather(x, axis, dim):
+    ways = lax.axis_size(axis)
+    up = [(d, (d + 1) % ways) for d in range(ways)]
+    down = [(d, (d - 1) % ways) for d in range(ways)]
+    earlier, later = ([x], [x])
+    for _ in range(ways // 2):
+        earlier.append(lax.ppermute(earlier[-1], axis, up))
+    for _ in range((ways - 1) // 2):
+        later.append(lax.ppermute(later[-1], axis, down))
+    line = jnp.concatenate([*earlier[::-1], *later[1:]], axis=dim)
+    return jnp.roll(line, (lax.axis_index(axis) - ways // 2) * x.shape[dim], axis=dim)
 
 
 def expert_backward(rows_x, rows_dy, gate_mat, up_mat, down_mat):
@@ -59,7 +72,7 @@
     got_x = lax.all_to_all(send_x, ("dp", "expert"), split_axis=0, concat_axis=0, tiled=True)
     got_dy = lax.all_to_all(send_dy, ("dp", "expert"), split_axis=0, concat_axis=0, tiled=True)
     got_x, got_dy = (
-        lax.all_gather(got_x, "head", axis=2, tiled=True),
+        ring_gather(got_x, "head", 2),
         lax.all_gather(got_dy, "head", axis=2, tiled=True),
     )
     sources = got_x.shape[0]

time: 201 us -> 190 us (0.945)
  blocking collectives: 33.3 us -> 25.3 us
  matrix products: 41.9 us -> 37 us
    all_gather x1 -> x0, blocking collectives: 9.47 us -> none  [expert_half(): lax.all_gather(got_x, 'head', axis=2, tiled=True)]
    dot_general x1, matrix products: 1.37 us -> 5.2 us  [expert_backward(): up_pre = jnp.dot(rows_x, up_mat, preferred_element_type=jnp.float32)]
    dot_general x1, matrix products: 5.54 us -> 2.31 us  [expert_backward(): lax.dot_general(d_pre, gate_mat, CONTRACT_LAST, preferred_element_type=jn...]
    dot_general x1, matrix products: 5.71 us -> 2.47 us  [expert_backward(): lax.dot_general(rows_dy, down_mat, CONTRACT_LAST, preferred_element_type=...]
    unnamed x35 -> x58, local copies, waits for them, and re-layouts: 8.81 us -> 8.81 us
  transfers between devices with their start and end apart: 7 -> 10, of which waited for: 2 -> 4; matrix products, arithmetic and copies ran while one was open for 52% -> 51% of each run, Pallas kernels for 0% -> 0%
where the time goes in v1:
time: 190 us; the launch traced here: 188 us
  other arithmetic  53.3 us (28%)
  matrix products  37 us (19%)
  starting transfers between devices  25.3 us (13%)
  blocking collectives  25.3 us (13%)
  local copies, waits for them, and re-layouts  24.7 us (13%)
  between operations  14.4 us (8%)
  waiting for transfers between devices  8.19 us (4%)
    gather x1, other arithmetic, expert_half(): jnp.take(flat_gate, safe_target)  40.1 us
    all_gather x1, blocking collectives, expert_half(): lax.all_gather(got_dy, 'head', axis=2, tiled=True)  11.1 us
    unnamed x58, local copies, waits for them, and re-layouts  8.81 us
    all_gather x1, blocking collectives, attention_half(): piece = lax.all_gather(latent_kv, 'expert', axis=0, tiled=True)  8.09 us
    all_to_all x1, starting transfers between devices, expert_half(): lax.all_to_all(send_x, ('dp', 'expert'), split_axis=0, concat_axis=0, til...  7.25 us
    unnamed x1, blocking collectives  6.15 us
    gather x1, local copies, waits for them, and re-layouts, expert_half(): jnp.take(flat_back, safe_target, axis=0).astype(jnp.float32)  5.81 us
    all_to_all x1, starting transfers between devices, expert_half(): lax.all_to_all(back_gate, ('dp', 'expert'), split_axis=0, concat_axis=0,...  5.8 us
  transfers between devices with their start and end apart: 10, of which 4 were waited for; matrix products, arithmetic and copies ran while one was open for 51% of the time, Pallas kernels for 0%

profile of v1, /device:TPU:0, one launch (start us, length us, event | category | flops | bytes accessed | tf_op | source)
XLA Modules:
  0.0 188.0 jit_solution(11775182257519535548)
XLA Ops:
  8.3 2.3 %reduce-window.6 = s32[8,8,128]{2,1,0:T(8,128)S(1)} reduce-window(s32[8,8,128]{2,1,0:T(8,128)S(1)} %fusion.41, s32[]{:T(128)} %constant.83.clone.1), window={size=1x1x128 pad=0_0x0_0x127_0}, to_apply=%region_0.1 | reduce-window | flops 1040384 | bytes 65540 | tf_op jit(solution)/shard_map/reduce-window
  13.9 7.3 %all-to-all-start.1 = ((bf16[8,8,1792]{2,1,0:T(8,128)(2,1)}), bf16[8,8,1792]{2,1,0:T(8,128)(2,1)S(1)}, u32[]{:S(2)}, u32[]{:S(2)}) async-start(bf16[8,8,1792]{2,1,0:T(8,128)(2,1)} %get-tuple-element.34), calls=%async_computation.1 | async-start | bytes 458752 | tf_op jit(solution)/shard_map/all_to_all | solution.py:72
  21.1 8.1 %all_gather.7 = bf16[256,576]{0,1:T(8,128)(2,1)S(1)} all-gather(bf16[128,576]{0,1:T(8,128)(2,1)} %param.22), channel_id=1, replica_groups=mesh['dp'=4,'expert'=2,'head'=4] {'expert'}, dimensions={0}, use_global_device_ids=true | all-gather | bytes 442368 | tf_op jit(solution)/shard_map/all_gather | solution.py:107
  35.2 3.6 %fusion.64 = (f32[8,256]{1,0:T(8,128)S(1)}, f32[8,256,256]{1,2,0:T(8,128)}) fusion(pred[256,256]{0,1:T(8,128)(4,1)S(1)} %fusion.33, bf16[256,8,192]{0,2,1:T(8,128)(2,1)} %bitcast.187, bf16[256,8,64]{0,2,1:T(8,128)(2,1)} %broadcast_in_dim.128, bf16[256,8,128]{0,2,1:T(8,128)(2,1)} %bitcast.190), kind=kOutput, calls=%fused_computation.186 | convolution fusion | flops 204996864 | bytes 3743744 | tf_op jit(solution)/shard_map/sub | solution.py:140
  38.7 4.1 %fusion.19 = bf16[256,8,192]{0,2,1:T(8,128)(2,1)} fusion(bf16[256,8,192]{0,2,1:T(8,128)(2,1)} %bitcast.188, f32[8,256,256]{2,1,0:T(8,128)S(1)} %fusion.65, f32[8,256,256]{1,2,0:T(8,128)} %get-tuple-element.102, f32[8,256]{1,0:T(8,128)S(1)} %get-tuple-element.101), kind=kOutput, calls=%fused_computation.33 | convolution fusion | flops 205392128 | bytes 5775360 | tf_op jit(solution)/shard_map/hqk,qhd->khd/dot_general | solution.py:153
  44.1 1.7 fusion.66
  47.1 4.7 %all-to-all-start = ((bf16[8,8,1792]{2,1,0:T(8,128)(2,1)}), bf16[8,8,1792]{2,1,0:T(8,128)(2,1)S(1)}, u32[]{:S(2)}, u32[]{:S(2)}) async-start(bf16[8,8,1792]{2,1,0:T(8,128)(2,1)} %get-tuple-element.33), calls=%async_computation | async-start | bytes 458752 | tf_op jit(solution)/shard_map/all_to_all | solution.py:73
  55.6 1.8 collective-permute-start.2
  60.2 11.1 %all_gather.6 = bf16[8,8,7168]{2,1,0:T(8,128)(2,1)S(1)} all-gather(bf16[8,8,1792]{2,1,0:T(8,128)(2,1)S(1)} %all-to-all-done), channel_id=1, replica_groups=mesh['dp'=4,'expert'=2,'head'=4] {'head'}, dimensions={2}, use_global_device_ids=true | all-gather | bytes 1146880 | tf_op jit(solution)/shard_map/all_gather | solution.py:76
  71.5 4.6 %fusion.4 = f32[64,512]{1,0:T(8,128)S(1)} fusion(bf16[1,7168,512]{2,1,0:T(8,128)(2,1)} %param.19, bf16[8,8,14336]{2,1,0:T(8,128)(2,1)S(1)} %constant_dynamic-update-slice_fusion, s32[]{:T(128)S(6)} %select_n.130), kind=kOutput, calls=%fused_computation.8 | convolution fusion | flops 469762048 | bytes 8388612 | tf_op jit(solution)/shard_map/dot_general | solution.py:30
  76.1 5.2 %fusion.7 = f32[64,512]{1,0:T(8,128)S(1)} fusion(bf16[1,7168,512]{2,1,0:T(8,128)(2,1)} %param.20, bf16[8,8,14336]{2,1,0:T(8,128)(2,1)S(1)} %constant_dynamic-update-slice_fusion, s32[]{:T(128)S(6)} %select_n.130), kind=kOutput, calls=%fused_computation.11 | convolution fusion | flops 469762048 | bytes 8388612 | tf_op jit(solution)/shard_map/dot_general | solution.py:31
  81.4 2.5 %multiply_reduce_fusion.1 = (f32[64]{0:T(128)S(1)}, f32[64,512]{1,0:T(8,128)S(1)}) fusion(f32[64,512]{1,0:T(8,128)S(1)} %fusion.7, f32[64,512]{1,0:T(8,128)S(1)} %fusion.4, bf16[1,512,7168]{2,1,0:T(8,128)(2,1)S(1)} %bitcast.180, bf16[8,8,7168]{2,1,0:T(8,128)(2,1)S(1)} %all_gather.6), kind=kOutput, calls=%fused_computation.62 | convolution fusion | flops 469991360 | bytes 8651008 | tf_op jit(solution)/shard_map/dot_general | solution.py:32
  83.9 2.3 %fusion.2 = f32[64,7168]{1,0:T(8,128)S(1)} fusion(bf16[1,7168,512]{2,1,0:T(8,128)(2,1)S(1)} %bitcast.178, f32[64,512]{1,0:T(8,128)S(1)} %fusion.4, f32[64,512]{1,0:T(8,128)S(1)} %get-tuple-element.100, f32[64,512]{1,0:T(8,128)S(1)} %fusion.7), kind=kOutput, calls=%fused_computation.6 | convolution fusion | flops 470089728 | bytes 9568256 | tf_op jit(solution)/shard_map/dot_general | solution.py:42
  86.2 3.6 %convolution_add_fusion = f32[64,7168]{1,0:T(8,128)} fusion(f32[64,7168]{1,0:T(8,128)S(1)} %fusion.2, bf16[1,7168,512]{2,1,0:T(8,128)(2,1)S(1)} %bitcast.176, f32[64,512]{1,0:T(8,128)S(1)} %get-tuple-element.100, f32[64,512]{1,0:T(8,128)S(1)} %fusion.4), kind=kOutput, calls=%fused_computation.5 | convolution fusion | flops 470417408 | bytes 11272192 | tf_op jit(solution)/shard_map/dot_general | solution.py:44
  91.1 4.3 %convolution_convert_fusion.2 = bf16[8,192,256]{2,1,0:T(8,128)(2,1)S(1)} fusion(f32[8,256,256]{2,1,0:T(8,128)} %copy-done.2, bf16[256,8,64]{0,2,1:T(8,128)(2,1)S(1)} %copy-done.10, bf16[256,8,128]{0,2,1:T(8,128)(2,1)S(1)} %bitcast.191, f32[8,256,256]{1,2,0:T(8,128)} %get-tuple-element.102, f32[8,256]{1,0:T(8,128)S(1)} %get-tuple-element.101), kind=kOutput, calls=%fused_computation.31 | convolution fusion | flops 206964992 | bytes 5775360 | tf_op jit(solution)/shard_map/hqk,khd->qhd/dot_general | solution.py:149
  95.5 6.2 %all-reduce = bf16[64,4]{0,1:T(4,128)(2,1)S(1)} all-reduce(f32[64,4]{0,1:T(4,128)S(1)} %broadcast_in_dim.125), channel_id=3, replica_groups=mesh['dp'=4,'expert'=2,'head'=4] {'head'}, use_global_device_ids=true, to_apply=%region_8.10.clone | all-reduce | flops 256 | bytes 1536
  103.0 5.8 %all-to-all-start.3 = ((bf16[8,1,8]{2,1,0:T(2,128)(2,1)}), bf16[8,1,8]{2,1,0:T(2,128)(2,1)S(1)}, u32[]{:S(2)}, u32[]{:S(2)}) async-start(bf16[8,1,8]{2,1,0:T(2,128)(2,1)} %convert_element_type.97), calls=%async_computation.4 | async-start | bytes 8192 | tf_op jit(solution)/shard_map/all_to_all | solution.py:90
  110.1 5.1 %all-to-all-done.3 = bf16[8,1,8]{2,1,0:T(2,128)(2,1)S(1)} async-done(((bf16[8,1,8]{2,1,0:T(2,128)(2,1)}), bf16[8,1,8]{2,1,0:T(2,128)(2,1)S(1)}, u32[]{:S(2)}, u32[]{:S(2)}) %all-to-all-start.3) | async-done | bytes 160 | tf_op jit(solution)/shard_map/all_to_all | solution.py:90
  118.2 1.8 copy.104
  120.3 1.7 convert_bitcast_fusion
  122.0 5.5 %all-to-all-start.2 = ((bf16[8,8,1792]{2,1,0:T(8,128)(2,1)}), bf16[8,8,1792]{2,1,0:T(8,128)(2,1)S(1)}, u32[]{:S(2)}, u32[]{:S(2)}) async-start(bf16[8,8,1792]{2,1,0:T(8,128)(2,1)} %convert_bitcast_fusion), calls=%async_computation.3 | async-start | bytes 458752 | tf_op jit(solution)/shard_map/all_to_all | solution.py:89
  127.5 40.1 %compare_select_fusion.2 = bf16[1024]{0:T(1024)(128)(2,1)S(1)} fusion(s32[1024]{0:T(1024)S(1)} %bitcast.195, bf16[]{:T(256)} %bitcast.13, bf16[]{:T(256)} %bitcast.14, bf16[]{:T(256)} %bitcast.15, bf16[]{:T(256)} %bitcast.16, bf16[]{:T(256)} %bitcast.17, bf16[]{:T(256)} %bitcast.18, bf16[]{:T(256)} %bitcast.19, bf16[]{:T(256)} %bitcast.20, bf16[]{:T(256)} %bitcast.21, ...), kind=kLoop, calls=%fused_computation.95 | loop fusion | flops 129024 | bytes 6272 | tf_op jit(solution)/shard_map/jit(_take)/gather | solution.py:98
  170.1 5.8 %gather_fusion = bf16[1024,1792]{1,0:T(8,128)(2,1)} fusion(bf16[64,1792]{1,0:T(8,128)(2,1)S(1)} %bitcast.174, s32[1024]{0:T(1024)S(1)} %broadcast_clamp_fusion), kind=kCustom, calls=%fused_computation.2 | custom fusion | bytes 7344128 | tf_op jit(solution)/shard_map/jit(_take)/gather | solution.py:96
  175.9 5.6 %multiply_reduce_fusion = bf16[128,1792]{1,0:T(8,128)(2,1)} fusion(bf16[1024,1792]{1,0:T(8,128)(2,1)} %gather_fusion, f32[128,8]{1,0:T(8,128)S(1)} %get-tuple-element.27, pred[128,8]{1,0:T(8,128)(4,1)S(1)} %get-tuple-element.26), kind=kLoop, calls=%fused_computation.15 | loop fusion | flops 7110656 | bytes 4133888 | tf_op jit(solution)/shard_map/reduce_sum | solution.py:97
  (125 shorter events, 29.0 us)
Async XLA Ops:
  7.2 4.2 %copy-start = (bf16[128,1792]{1,0:T(8,128)(2,1)S(1)}, bf16[128,1792]{1,0:T(8,128)(2,1)}, u32[]{:S(2)}) copy-start(bf16[128,1792]{1,0:T(8,128)(2,1)} %param.16) | copy-start | bytes 1376260
  7.2 5.0 %copy-start.1 = (bf16[128,1792]{1,0:T(8,128)(2,1)S(1)}, bf16[128,1792]{1,0:T(8,128)(2,1)}, u32[]{:S(2)}) copy-start(bf16[128,1792]{1,0:T(8,128)(2,1)} %param.15) | copy-start | bytes 1376260
  12.2 17.0 %copy-start.3 = (bf16[512,1024]{1,0:T(8,128)(2,1)S(1)}, bf16[512,1024]{1,0:T(8,128)(2,1)}, u32[]{:S(2)}) copy-start(bf16[512,1024]{1,0:T(8,128)(2,1)} %param.25) | copy-start | bytes 3145732
  12.2 17.0 %copy-start.4 = (bf16[512,1024]{1,0:T(8,128)(2,1)S(1)}, bf16[512,1024]{1,0:T(8,128)(2,1)}, u32[]{:S(2)}) copy-start(bf16[512,1024]{1,0:T(8,128)(2,1)} %param.26) | copy-start | bytes 3145732
  13.9 33.3 %all-to-all-start.1 = ((bf16[8,8,1792]{2,1,0:T(8,128)(2,1)}), bf16[8,8,1792]{2,1,0:T(8,128)(2,1)S(1)}, u32[]{:S(2)}, u32[]{:S(2)}) async-start(bf16[8,8,1792]{2,1,0:T(8,128)(2,1)} %get-tuple-element.34), calls=%async_computation.1 | async-start | bytes 458752 | tf_op jit(solution)/shard_map/all_to_all | solution.py:72
  31.7 2.7 %slice-start.6 = ((bf16[256,576]{0,1:T(8,128)(2,1)}), bf16[256,64]{0,1:T(8,128)(2,1)S(1)}, s32[]{:S(2)}) async-start(bf16[256,576]{0,1:T(8,128)(2,1)} %copy-done.9), calls=%async_computation.16 | async-start | bytes 65536 | tf_op jit(solution)/shard_map/slice | solution.py:111
  34.4 4.4 %copy-start.2 = (f32[8,256,256]{2,1,0:T(8,128)}, f32[8,256,256]{2,1,0:T(8,128)S(1)}, u32[]{:S(2)}) copy-start(f32[8,256,256]{2,1,0:T(8,128)S(1)} %fusion.65) | copy-start | bytes 6291460
  42.9 2.9 %copy-start.14 = (f32[8,256,256]{1,2,0:T(8,128)S(1)}, f32[8,256,256]{1,2,0:T(8,128)}, u32[]{:S(2)}) copy-start(f32[8,256,256]{1,2,0:T(8,128)} %get-tuple-element.102) | copy-start | bytes 6291460
  45.8 6.1 %copy-start.5 = (bf16[512,1024]{1,0:T(8,128)(2,1)S(1)}, bf16[512,1024]{1,0:T(8,128)(2,1)}, u32[]{:S(2)}) copy-start(bf16[512,1024]{1,0:T(8,128)(2,1)} %param.26) | copy-start | bytes 3145732
  47.1 13.1 %all-to-all-start = ((bf16[8,8,1792]{2,1,0:T(8,128)(2,1)}), bf16[8,8,1792]{2,1,0:T(8,128)(2,1)S(1)}, u32[]{:S(2)}, u32[]{:S(2)}) async-start(bf16[8,8,1792]{2,1,0:T(8,128)(2,1)} %get-tuple-element.33), calls=%async_computation | async-start | bytes 458752 | tf_op jit(solution)/shard_map/all_to_all | solution.py:73
  51.9 66.3 %reduce-scatter.8.cloned.1.call-start = ((), (), s32[]{:S(2)}) async-start(), calls=%async_computation.8 | async-start | bytes 983040 | tf_op jit(solution)/shard_map/reduce_scatter | solution.py:173
  53.5 5.5 %collective-permute-start = (bf16[8,8,1792]{2,1,0:T(8,128)(2,1)S(1)}, bf16[8,8,1792]{2,1,0:T(8,128)(2,1)S(1)}, u32[]{:S(2)}, u32[]{:S(2)}) collective-permute-start(bf16[8,8,1792]{2,1,0:T(8,128)(2,1)S(1)} %all-to-all-done.1), channel_id=1, source_target_pairs={{0,1},{1,2},{2,3},{3,0},{4,5},{5,6},{6,7},{7,4},{8,9},{9,10},{10,1... | collective-permute-start | bytes 688136 | tf_op jit(solution)/shard_map/ppermute | solution.py:22
  55.5 64.7 %reduce-scatter.6.cloned.1.call-start = ((), (), s32[]{:S(2)}) async-start(), calls=%async_computation.7 | async-start | bytes 2293760 | tf_op jit(solution)/shard_map/reduce_scatter | solution.py:84
  55.6 15.7 %collective-permute-start.2 = (bf16[8,8,1792]{2,1,0:T(8,128)(2,1)S(1)}, bf16[8,8,1792]{2,1,0:T(8,128)(2,1)S(1)}, u32[]{:S(2)}, u32[]{:S(2)}) collective-permute-start(bf16[8,8,1792]{2,1,0:T(8,128)(2,1)S(1)} %all-to-all-done.1), channel_id=1, source_target_pairs={{0,3},{1,0},{2,1},{3,2},{4,7},{5,4},{6,5},{7,6},{8,11},{9,8},{10,9... | collective-permute-start | bytes 688136 | tf_op jit(solution)/shard_map/ppermute | solution.py:24
  59.0 12.3 %collective-permute-start.1 = (bf16[8,8,1792]{2,1,0:T(8,128)(2,1)S(1)}, bf16[8,8,1792]{2,1,0:T(8,128)(2,1)S(1)}, u32[]{:S(2)}, u32[]{:S(2)}) collective-permute-start(bf16[8,8,1792]{2,1,0:T(8,128)(2,1)S(1)} %collective-permute-done), channel_id=1, source_target_pairs={{0,1},{1,2},{2,3},{3,0},{4,5},{5,6},{6,7},{7,4},{8,9},{9,10},{10,1... | collective-permute-start | bytes 688136 | tf_op jit(solution)/shard_map/ppermute | solution.py:22
  71.4 9.9 %slice-start.4 = ((s8[7340032]{0:T(1024)(128)(4,1)}), s8[4194304]{0:T(1024)(128)(4,1)S(1)}, s32[]{:S(2)}) async-start(s8[7340032]{0:T(1024)(128)(4,1)} %bitcast.179), calls=%async_computation.14 | async-start | bytes 8388608
  71.5 9.9 %slice-start.5 = ((s8[7340032]{0:T(1024)(128)(4,1)}), s8[3145728]{0:T(1024)(128)(4,1)S(1)}, s32[]{:S(2)}) async-start(s8[7340032]{0:T(1024)(128)(4,1)} %bitcast.179), calls=%async_computation.15 | async-start | bytes 6291456
  71.5 12.4 %slice-start.2 = ((s8[7340032]{0:T(1024)(128)(4,1)}), s8[4194304]{0:T(1024)(128)(4,1)S(1)}, s32[]{:S(2)}) async-start(s8[7340032]{0:T(1024)(128)(4,1)} %bitcast.177), calls=%async_computation.12 | async-start | bytes 8388608
  76.1 7.8 %slice-start.3 = ((s8[7340032]{0:T(1024)(128)(4,1)}), s8[3145728]{0:T(1024)(128)(4,1)S(1)}, s32[]{:S(2)}) async-start(s8[7340032]{0:T(1024)(128)(4,1)} %bitcast.177), calls=%async_computation.13 | async-start | bytes 6291456
  81.4 4.8 %slice-start = ((s8[7340032]{0:T(1024)(128)(4,1)}), s8[4194304]{0:T(1024)(128)(4,1)S(1)}, s32[]{:S(2)}) async-start(s8[7340032]{0:T(1024)(128)(4,1)} %bitcast.175), calls=%async_computation.10 | async-start | bytes 8388608
  86.2 3.7 %copy-start.11 = (f32[128,8]{0,1:T(8,128)S(1)}, f32[128,8]{0,1:T(8,128)}, u32[]{:S(2)}) copy-start(f32[128,8]{0,1:T(8,128)} %param.18) | copy-start | bytes 12292
  103.0 12.2 %all-to-all-start.3 = ((bf16[8,1,8]{2,1,0:T(2,128)(2,1)}), bf16[8,1,8]{2,1,0:T(2,128)(2,1)S(1)}, u32[]{:S(2)}, u32[]{:S(2)}) async-start(bf16[8,1,8]{2,1,0:T(2,128)(2,1)} %convert_element_type.97), calls=%async_computation.4 | async-start | bytes 8192 | tf_op jit(solution)/shard_map/all_to_all | solution.py:90
  108.8 59.7 %reduce-scatter.10.cloned.1.call-start = ((), (), s32[]{:S(2)}) async-start(), calls=%async_computation.9 | async-start | bytes 368640
  122.0 48.1 %all-to-all-start.2 = ((bf16[8,8,1792]{2,1,0:T(8,128)(2,1)}), bf16[8,8,1792]{2,1,0:T(8,128)(2,1)S(1)}, u32[]{:S(2)}, u32[]{:S(2)}) async-start(bf16[8,8,1792]{2,1,0:T(8,128)(2,1)} %convert_bitcast_fusion), calls=%async_computation.3 | async-start | bytes 458752 | tf_op jit(solution)/shard_map/all_to_all | solution.py:89
  (8 other events, 10.4 us)
Sparse Core Ops, SparseCore 0:
  55.7 17.6 reduce-scatter.7
  90.0 30.2 reduce-scatter.5
  123.3 20.2 reduce-scatter.9
